TPU v7x, 256 devices: a whole 4x4x8 slice. The times are simulated.
256 devices in a mesh: grp: 16 (over x, y), rank: 16 (over z, core).
Axes of the slice: x: 4, y: 4, z: 8, core: 2. Of those that a mesh axis runs over, the one named last changes fastest.
Arguments:
- queries: bfloat16 [2048, 64, 576], P(('grp', 'rank')), parts along dimension 0, may hold values from -64 to 64
- cache_pool: bfloat16 [4096, 64, 576], P(('grp', 'rank')), parts along dimension 0, may hold values from -6 to 6
- page_table: int32 [2048, 2], P(('grp', 'rank')), parts along dimension 0, may hold values from 0 to 15, as said below
- lengths: int32 [2048], P(('grp', 'rank')), parts along dimension 0, may hold values from 1 to 128, as said below
- residual: bfloat16 [2048, 3584], P(('grp', 'rank')), parts along dimension 0, may hold values from -3 to 3
- w_uv: bfloat16 [64, 512, 128], P('rank'), may hold values from -1 to 1
- w_out: bfloat16 [8192, 3584], P('rank'), may hold values from -0.125 to 0.125
- norm_gain: float32 [3584], replicated, may hold values from 0.1 to 1.9
- w_gate: bfloat16 [3584, 9216], P(None, 'rank'), may hold values from -0.09375 to 0.09375
- w_down: bfloat16 [9216, 3584], P('rank'), may hold values from -0.125 to 0.125
Outputs:
- attended: bfloat16 [2048, 3584], P(('grp', 'rank')), parts along dimension 0
- ffn_out: bfloat16 [2048, 3584], P(('grp', 'rank')), parts along dimension 0
There are 16 independent parts, one for each index of `grp`. A program takes and returns all parts, laid end to end along the dimension named above; an argument that names none is the same for every part. Nothing has to cross between parts.
Inputs may be any that keep to these rules, and one draw needn't show every extreme that they name: `lengths`: each row's live positions lie at its start; in every group some row holds exactly 128. `page_table`: the rows of one rank use each of that rank's 16 pages exactly once.
All inputs are finite; a program needn't handle non-finite values.
Results may differ from a plain program's by a relative error of at most 0.02.
Values may be sent and summed in bfloat16 or wider, within the bound.
A program may use at most 64 MiB of HBM per device.

v0:
```python
import jax
import jax.numpy as jnp
from jax import lax
from jax.sharding import PartitionSpec as P

LAT = 512


score_scale = 0.07216878364870322


def attend(queries, cache_pool, page_table, lengths):
    num_rows = queries.shape[0]
    key_rows = cache_pool[page_table].reshape(num_rows, -1, cache_pool.shape[2])
    cache_len = key_rows.shape[1]
    scores = (
        jnp.einsum("bhk,btk->bht", queries, key_rows, preferred_element_type=jnp.float32)
        * score_scale
    )
    is_valid = jnp.arange(cache_len, dtype=jnp.int32)[None, None, :] < lengths[:, None, None]
    scores = jnp.where(is_valid, scores, jnp.float32(-1e30))
    weights = jax.nn.softmax(scores, axis=-1).astype(jnp.bfloat16)
    context = jnp.einsum(
        "bht,btl->bhl", weights, key_rows[:, :, :LAT], preferred_element_type=jnp.float32
    )
    return context.astype(jnp.bfloat16)


def body(
    queries, cache_pool, page_table, lengths, residual, w_uv, w_out, norm_gain, w_gate, w_down
):
    context = attend(queries, cache_pool, page_table, lengths)
    by_heads = lax.all_to_all(context, "rank", split_axis=1, concat_axis=0, tiled=True)
    values = jnp.einsum("bhl,hlv->bhv", by_heads, w_uv, preferred_element_type=jnp.float32)
    values = values.astype(jnp.bfloat16).reshape(by_heads.shape[0], -1)
    attn_part = jnp.dot(values, w_out, preferred_element_type=jnp.float32)
    attn_sum = lax.psum_scatter(attn_part, "rank", scatter_dimension=0, tiled=True)
    attended = (residual.astype(jnp.float32) + attn_sum).astype(jnp.bfloat16)
    wide = attended.astype(jnp.float32)
    mean_square = jnp.mean(wide * wide, axis=-1, keepdims=True)
    normed = (wide / jnp.sqrt(mean_square + 1e-06) * norm_gain).astype(jnp.bfloat16)
    gathered = lax.all_gather(normed, "rank", axis=0, tiled=True)
    hidden = jax.nn.silu(jnp.dot(gathered, w_gate, preferred_element_type=jnp.float32)).astype(
        jnp.bfloat16
    )
    partial_value = jnp.dot(hidden, w_down, preferred_element_type=jnp.float32)
    ffn_sum = lax.psum_scatter(
        partial_value.astype(jnp.bfloat16), "rank", scatter_dimension=0, tiled=True
    ).astype(jnp.float32)
    ffn_out = (wide + ffn_sum).astype(jnp.bfloat16)
    return (attended, ffn_out)


def solution(mesh):
    return jax.shard_map(
        body,
        mesh=mesh,
        in_specs=(
            P(("grp", "rank"), None, None),
            P(("grp", "rank"), None, None),
            P(("grp", "rank"), None),
            P(("grp", "rank")),
            P(("grp", "rank"), None),
            P("rank", None, None),
            P("rank", None),
            P(),
            P(None, "rank"),
            P("rank", None),
        ),
        out_specs=(P(("grp", "rank"), None), P(("grp", "rank"), None)),
        check_vma=False,
    )
```

profile of v0, /device:TPU:1, one launch (start us, length us, event | category | flops | bytes accessed | tf_op | source)
XLA Modules:
  0.0 188.4 jit_solution(15102598867705543306)
XLA Ops:
  7.2 0.0 copy-start
  7.2 0.0 copy-start.1
  7.2 0.0 reduce-scatter.3.cloned.1.call-start
  7.2 0.8 compare_select_fusion
  8.0 0.7 iota_compare_fusion
  8.8 0.1 copy.20
  8.9 0.1 reshape.46
  8.9 0.0 copy-done
  9.0 0.8 gather_fusion
  9.7 0.0 copy-done.1
  9.8 0.6 fusion.4
  10.4 0.2 fusion.16
  10.6 0.0 copy-start.2
  10.7 1.8 convolution_convert_fusion.1
  12.5 1.3 copy.22
  13.8 27.1 %all_to_all.18 = bf16[8,64,512]{2,0,1:T(8,128)(2,1)S(1)} all-to-all(bf16[8,64,512]{2,0,1:T(8,128)(2,1)S(1)} %copy.22), channel_id=1, replica_groups=mesh['grp'=16,'rank'=16] {'rank'}, dimensions={1} | all-to-all | bytes 1048576 | tf_op jit(solution)/shard_map/all_to_all | solution.py:33
  40.9 0.0 copy-done.2
  40.9 0.3 convolution_convert_fusion.2
  41.3 4.0 %fusion.19 = f32[128,3584]{1,0:T(8,128)} fusion(bf16[128,512]{0,1:T(8,128)(2,1)S(1)} %bitcast.25, bf16[512,3584]{1,0:T(8,128)(2,1)} %param.16), kind=kOutput, calls=%fused_computation.33 | convolution fusion | flops 469762048 | bytes 5636096 | tf_op jit(solution)/shard_map/dot_general | solution.py:36
  45.2 0.0 reduce-scatter.3.cloned.1.call-update
  45.3 0.0 reduce-scatter.5.cloned.1.call-start
  45.3 52.5 %reduce-scatter.3.cloned.1.call-done = f32[8,3584]{1,0:T(8,128)} async-done(((f32[128,3584]{1,0:T(8,128)}), f32[8,3584]{1,0:T(8,128)}) %reduce-scatter.3.cloned.1.call-update) | async-done | bytes 114704 | tf_op jit(solution)/shard_map/reduce_scatter | solution.py:37
  97.8 0.0 copy-done.4
  97.8 1.0 fusion.10
  98.9 0.0 copy-done.5
  98.9 0.1 fusion.12
  99.0 20.6 %all_gather.3 = bf16[128,3584]{1,0:T(8,128)(2,1)S(1)} all-gather(bf16[8,3584]{1,0:T(8,128)(2,1)S(1)} %fusion.12), channel_id=1, replica_groups=mesh['grp'=16,'rank'=16] {'rank'}, dimensions={0}, use_global_device_ids=true | all-gather | bytes 974848 | tf_op jit(solution)/shard_map/all_gather | solution.py:42
  119.5 7.8 %convolution_convert_fusion = bf16[128,3584]{1,0:T(8,128)(2,1)} fusion(bf16[576,3584]{1,0:T(8,128)(2,1)} %param.19, bf16[128,3584]{1,0:T(8,128)(2,1)S(1)} %all_gather.3, bf16[3584,576]{0,1:T(8,128)(2,1)} %param.18), kind=kOutput, calls=%fused_computation.2 | convolution fusion | flops 1057792000 | bytes 10092544 | tf_op jit(solution)/shard_map/dot_general | solution.py:46
  127.3 0.0 reduce-scatter.5.cloned.1.call-update
  127.4 52.7 %reduce-scatter.5.cloned.1.call-done = bf16[8,3584]{1,0:T(8,128)(2,1)} async-done(((bf16[128,3584]{1,0:T(8,128)(2,1)}), bf16[8,3584]{1,0:T(8,128)(2,1)}) %reduce-scatter.5.cloned.1.call-update) | async-done | bytes 57360 | tf_op jit(solution)/shard_map/reduce_scatter | solution.py:47
  180.1 0.0 copy-done.3
  180.1 1.5 fusion.13
  (5 shorter events, 0.0 us)
Async XLA Ops:
  7.2 1.8 copy-start
  7.2 2.6 %copy-start.1 = (bf16[8,64,576]{2,1,0:T(8,128)(2,1)S(1)}, bf16[8,64,576]{2,1,0:T(8,128)(2,1)}, u32[]{:S(2)}) copy-start(bf16[8,64,576]{2,1,0:T(8,128)(2,1)} %param.10) | copy-start | bytes 1769476
  7.2 90.6 %reduce-scatter.3.cloned.1.call-start = ((), (), s32[]{:S(2)}) async-start(), calls=%async_computation.3 | async-start | bytes 1949696 | tf_op jit(solution)/shard_map/reduce_scatter | solution.py:37
  10.6 30.3 %copy-start.2 = (bf16[4,512,128]{2,1,0:T(8,128)(2,1)S(1)}, bf16[4,512,128]{2,1,0:T(8,128)(2,1)}, u32[]{:S(2)}) copy-start(bf16[4,512,128]{2,1,0:T(8,128)(2,1)} %param.15) | copy-start | bytes 1572868
  45.2 52.6 %copy-start.4 = (bf16[8,3584]{1,0:T(8,128)(2,1)S(1)}, bf16[8,3584]{1,0:T(8,128)(2,1)}, u32[]{:S(2)}) copy-start(bf16[8,3584]{1,0:T(8,128)(2,1)} %param.14) | copy-start | bytes 172036
  45.2 53.6 %copy-start.5 = (f32[3584]{0:T(1024)S(1)}, f32[3584]{0:T(1024)}, u32[]{:S(2)}) copy-start(f32[3584]{0:T(1024)} %param.17) | copy-start | bytes 43012
  45.3 134.8 %reduce-scatter.5.cloned.1.call-start = ((), (), s32[]{:S(2)}) async-start(), calls=%async_computation.4 | async-start | bytes 974848 | tf_op jit(solution)/shard_map/reduce_scatter | solution.py:47
  98.8 81.2 %copy-start.3 = (bf16[8,3584]{1,0:T(8,128)(2,1)}, bf16[8,3584]{1,0:T(8,128)(2,1)S(1)}, u32[]{:S(2)}) copy-start(bf16[8,3584]{1,0:T(8,128)(2,1)S(1)} %get-tuple-element.3) | copy-start | bytes 172036
Sparse Core Ops, SparseCore 0:
  45.4 52.3 reduce-scatter.2
  127.5 52.5 reduce-scatter.4
where the time goes:
time: 191 us; the launch traced here: 188 us
  waiting for transfers between devices  105 us (55%)
  blocking collectives  47.7 us (25%)
  matrix products  14.6 us (8%)
  between operations  14.1 us (7%)
  other arithmetic  4.38 us (2%)
  local copies, waits for them, and re-layouts  2.31 us (1%)
    reduce_scatter x1, waiting for transfers between devices, body(): lax.psum_scatter(partial_value.astype(jnp.bfloat16), 'rank', scatter_dime...  52.7 us
    reduce_scatter x1, waiting for transfers between devices, body(): lax.psum_scatter(attn_part, 'rank', scatter_dimension=0, tiled=True)  52.5 us
    all_to_all x1, blocking collectives, body(): lax.all_to_all(context, 'rank', split_axis=1, concat_axis=0, tiled=True)  27.1 us
    all_gather x1, blocking collectives, body(): gathered = lax.all_gather(normed, 'rank', axis=0, tiled=True)  20.6 us
    dot_general x1, matrix products, body(): partial_value = jnp.dot(hidden, w_down, preferred_element_type=jnp.float32)  7.79 us
    dot_general x1, matrix products, body(): attn_part = jnp.dot(values, w_out, preferred_element_type=jnp.float32)  3.97 us
  transfers between devices with their start and end apart: 2, of which 2 were waited for; matrix products, arithmetic and copies ran while one was open for 0% of the time, Pallas kernels for 0%

commit v1 on v0

v1 whole, which is shorter than its diff:
```python
import jax
import jax.numpy as jnp
from jax import lax
from jax.experimental import pallas as pl
from jax.experimental.pallas import tpu as pltpu
from jax.sharding import PartitionSpec as P

SCALE = 0.07216878364870322
LAT = 512
KW = 576
D = 3584
HALF = 1792
CH = 896
FFL = 576
Z = 8
BF = jnp.bfloat16
F32 = jnp.float32
MESH = pl.DeviceIdType.MESH

PIECES = [(d, k, dist) for d in (0, 1) for k in (0, 1) for dist in (4, 3, 2, 1) if dist < 4 or d == k]
PIX = {p: i for i, p in enumerate(PIECES)}
NP = len(PIECES)


def kernel(
    q_h, pool_h, pt, ln, res_h, wuv_h, wout_h, gain_h, wg_h, wd_h,
    att_o, ffn_o,
    qv, poolv, resv, wuvv, woutv, gainv, wgv, wdv,
    sctx, ctxb, rctx, lhs, vals,
    part, pss, psr, rsb, rrb, gown, goth, xin, sq, hid, res_s, res_r, att16, fin_s, fin_r, outx_s, outx_r,
    lsem, a2a_s, a2a_r, ps_ss, ps_rs, rg_ss, rg_rs, ag_ss, ag_rs, sb_ss, sb_rs, ex_ss, ex_rs,
):
    me = lax.axis_index("rank")
    z = lax.div(me, 2)
    c = lax.rem(me, 2)
    sib = me + 1 - 2 * c

    def chip(j):
        return lax.rem(z + j, Z)

    down = {"rank": chip(7) * 2 + c}
    up = {"rank": chip(1) * 2 + c}
    other = {"rank": sib}

    own_col = pl.multiple_of(c * HALF, 128)
    oth_col = pl.multiple_of((1 - c) * HALF, 128)

    copies = []

    def load(src, dst):
        cp = pltpu.make_async_copy(src, dst, lsem.at[len(copies)])
        copies.append(cp)
        cp.start()
        return cp

    l_q = load(q_h, qv)
    l_pool = load(pool_h, poolv)
    l_res = load(res_h, resv)
    l_wuv = load(wuv_h, wuvv)
    l_wout = [load(wout_h.at[:, pl.ds(o, HALF)], woutv.at[i]) for i, o in enumerate((oth_col, own_col))]
    l_gain = [load(gain_h.at[:, pl.ds(o, HALF)], gainv.at[i]) for i, o in enumerate((oth_col, own_col))]
    l_wg = [load(wg_h.at[pl.ds(o, HALF), :], wgv.at[i]) for i, o in enumerate((oth_col, own_col))]
    l_wd = [load(wd_h.at[:, pl.ds(o, HALF)], wdv.at[i]) for i, o in enumerate((oth_col, own_col))]

    barrier = pltpu.get_barrier_semaphore()
    for k in range(1, 16):
        pl.semaphore_signal(barrier, inc=1, device_id={"rank": lax.rem(me + k, 16)}, device_id_type=MESH)

    l_q.wait()
    l_pool.wait()
    col = lax.broadcasted_iota(jnp.int32, (64, 128), 1)
    for b in range(8):
        key = jnp.concatenate([poolv[pt[b, 0]], poolv[pt[b, 1]]], axis=0)
        s = lax.dot_general(qv[b], key, (((1,), (1,)), ((), ())), preferred_element_type=F32) * SCALE
        s = jnp.where(col < ln[b], s, F32(-1e30))
        p = jnp.exp(s - jnp.max(s, axis=-1, keepdims=True))
        w = (p / jnp.sum(p, axis=-1, keepdims=True)).astype(BF)
        ctx = jnp.dot(w, key[:, :LAT], preferred_element_type=F32)
        for i in range(4):
            sctx[i, pl.ds(b, 64, stride=8), :] = ctx[:, i * 128 : (i + 1) * 128]
    for i in range(4):
        ctxb[:, pl.ds(i * 128, 128)] = sctx[i].astype(BF)

    pl.semaphore_wait(barrier, 15)

    sends = []

    def remote(src, dst, ss, rs, dev):
        cp = pltpu.make_async_remote_copy(
            src_ref=src, dst_ref=dst, send_sem=ss, recv_sem=rs, device_id=dev, device_id_type=MESH
        )
        cp.start()
        sends.append(cp)
        return cp

    def arrived(dst, rs):
        pltpu.make_async_copy(dst, dst, rs).wait()

    for j in (4, 3, 5, 2, 6, 1, 7):
        for k in (0, 1):
            dst = chip(j) * 2 + k
            remote(
                ctxb.at[pl.ds(pl.multiple_of(dst * 32, 32), 32), :],
                rctx.at[(8 - j) % 8, c],
                a2a_s.at[j, k],
                a2a_r.at[(8 - j) % 8, c],
                {"rank": dst},
            )
    remote(
        ctxb.at[pl.ds(pl.multiple_of(sib * 32, 32), 32), :],
        rctx.at[0, c],
        a2a_s.at[0, 0],
        a2a_r.at[0, c],
        other,
    )
    rctx[0, c] = ctxb[pl.ds(pl.multiple_of(me * 32, 32), 32), :]

    l_res.wait()
    res_r[c] = resv[:, pl.ds(own_col, HALF)].astype(F32)
    res_s[...] = resv[:, pl.ds(oth_col, HALF)].astype(F32)
    remote(res_s, res_r.at[c], ex_ss.at[0], ex_rs.at[0], other)

    def unpack(j):
        for hp in (0, 1):
            lo = rctx[j, 0, pl.ds(hp * 16, 16), :].astype(F32)
            hi = rctx[j, 1, pl.ds(hp * 16, 16), :].astype(F32)
            for h in (0, 1):
                blk = jnp.concatenate([lo[h * 8 : h * 8 + 8], hi[h * 8 : h * 8 + 8]], axis=0)
                lhs[hp * 2 + h, pl.ds(j * 16, 16), :] = blk.astype(BF)

    arrived(rctx.at[0, 1 - c], a2a_r.at[0, 1 - c])
    unpack(0)
    for j in (1, 7, 2, 6, 3, 5, 4):
        for k in (0, 1):
            arrived(rctx.at[j, k], a2a_r.at[j, k])
        unpack(j)

    l_wuv.wait()
    for h in range(4):
        v = jnp.dot(lhs[h], wuvv[h], preferred_element_type=F32)
        vals[:, pl.ds(h * 128, 128)] = v.astype(BF)

    def reduce_scatter(t, left, weights, loads):
        for w in loads:
            w.wait()
        for k in (0, 1):
            o = jnp.dot(left[...], weights[0, :, pl.ds(k * CH, CH)], preferred_element_type=F32)
            pss[t, k] = o.astype(BF)
            remote(pss.at[t, k], psr.at[t, k], ps_ss.at[t, k], ps_rs.at[t, k], other)
        for k in (0, 1):
            part[k] = jnp.dot(left[...], weights[1, :, pl.ds(k * CH, CH)], preferred_element_type=F32)

        def chip_sum(k, slot):
            rows = pl.ds(slot * 16, 16)
            return part[k, rows, :] + psr[t, k, rows, :].astype(F32)

        def step(d, k, dist):
            i = PIX[(d, k, dist)]
            slot = (8 - dist) if d == 0 else dist
            acc = chip_sum(k, slot)
            if (d, k, dist + 1) in PIX:
                prev = PIX[(d, k, dist + 1)]
                arrived(rrb.at[t, prev], rg_rs.at[t, prev])
                acc = acc + rrb[t, prev].astype(F32)
            rsb[t, i] = acc.astype(BF)
            remote(rsb.at[t, i], rrb.at[t, i], rg_ss.at[t, i], rg_rs.at[t, i], down if d == 0 else up)

        arrived(psr.at[t, 0], ps_rs.at[t, 0])
        step(0, 0, 4)
        step(1, 0, 3)
        arrived(psr.at[t, 1], ps_rs.at[t, 1])
        step(1, 1, 4)
        step(0, 1, 3)
        for dist in (3, 2, 1):
            step(0, 0, dist)
            step(1, 1, dist)
            if dist > 1:
                step(1, 0, dist - 1)
                step(0, 1, dist - 1)
        out = []
        for k in (0, 1):
            acc = chip_sum(k, 0)
            for d in ((1, 0) if k == 0 else (0, 1)):
                i = PIX[(d, k, 1)]
                arrived(rrb.at[t, i], rg_rs.at[t, i])
                acc = acc + rrb[t, i].astype(F32)
            out.append(acc)
        return out

    attn = reduce_scatter(0, vals, woutv, l_wout)

    arrived(res_r.at[1 - c], ex_rs.at[0])
    for w in l_gain:
        w.wait()

    def prepare(src, half, slot, k):
        cols = pl.ds(k * CH, CH)
        rows = pl.ds(slot * 16, 16)
        v = src.astype(F32)
        xin[half, rows, cols] = (v * gainv[half, :, cols]).astype(BF)
        s = v * v
        tot = s[:, 0:128]
        for i in range(1, CH // 128):
            tot = tot + s[:, i * 128 : (i + 1) * 128]
        sq[rows, :] = sq[rows, :] + tot

    sq[...] = jnp.zeros_like(sq)

    def to_sibling(slot, k):
        remote(gown.at[slot, k], goth.at[slot, k], sb_ss.at[slot, k], sb_rs.at[slot, k], other)

    def forward(d, k, dist):
        if (d, k, dist) not in PIX:
            return
        i = PIX[(d, k, dist)]
        src = (dist - 1) if d == 0 else (9 - dist) % 8
        dst = dist if d == 0 else 8 - dist
        remote(gown.at[src, k], gown.at[dst, k], ag_ss.at[i], ag_rs.at[i], down if d == 0 else up)

    for k in (0, 1):
        res = jnp.concatenate([res_r[0, :, k * CH : (k + 1) * CH], res_r[1, :, k * CH : (k + 1) * CH]], axis=0)
        att = (attn[k] + res).astype(BF)
        gown[0, k] = att
        forward(0, k, 1)
        forward(1, k, 1)
        to_sibling(0, k)
        att16[:, pl.ds(k * CH, CH)] = att.astype(F32)
    outx_s[0] = att16[pl.ds(pl.multiple_of((1 - c) * 8, 8), 8), :]
    remote(outx_s.at[0], outx_r.at[0], ex_ss.at[1], ex_rs.at[1], other)
    for k in (0, 1):
        prepare(gown[0, k], 1, 0, k)

    for dist in (1, 2, 3, 4):
        for k in (0, 1):
            for d in (0, 1):
                if (d, k, dist) not in PIX:
                    continue
                i = PIX[(d, k, dist)]
                slot = dist if d == 0 else 8 - dist
                arrived(gown.at[slot, k], ag_rs.at[i])
                forward(d, k, dist + 1)
                to_sibling(slot, k)
                prepare(gown[slot, k], 1, slot, k)
        for slot in sorted({dist - 1, (9 - dist) % 8}):
            for k in (0, 1):
                arrived(goth.at[slot, k], sb_rs.at[slot, k])
                prepare(goth[slot, k], 0, slot, k)
    for w in l_wg:
        w.wait()
    acc = jnp.dot(xin[1], wgv[1], preferred_element_type=F32)
    for k in (0, 1):
        arrived(goth.at[4, k], sb_rs.at[4, k])
        prepare(goth[4, k], 0, 4, k)
    acc = acc + jnp.dot(xin[0], wgv[0], preferred_element_type=F32)
    inv = lax.rsqrt(jnp.sum(sq[...], axis=-1, keepdims=True) * F32(1.0 / D) + F32(1e-6))
    g = acc * inv
    hid[...] = (g / (1.0 + jnp.exp(-g))).astype(BF)

    ffn = reduce_scatter(1, hid, wdv, l_wd)
    for k in (0, 1):
        cols = pl.ds(k * CH, CH)
        fin_s[:, cols] = (att16[:, cols] + ffn[k]).astype(BF).astype(F32)
    outx_s[1] = fin_s[pl.ds(pl.multiple_of((1 - c) * 8, 8), 8), :]
    remote(outx_s.at[1], outx_r.at[1], ex_ss.at[2], ex_rs.at[2], other)
    mine = pl.ds(pl.multiple_of(c * 8, 8), 8)
    att_o[:, pl.ds(own_col, HALF)] = att16[mine, :].astype(BF)
    ffn_o[:, pl.ds(own_col, HALF)] = fin_s[mine, :].astype(BF)
    arrived(outx_r.at[0], ex_rs.at[1])
    att_o[:, pl.ds(oth_col, HALF)] = outx_r[0].astype(BF)
    arrived(outx_r.at[1], ex_rs.at[2])
    ffn_o[:, pl.ds(oth_col, HALF)] = outx_r[1].astype(BF)
    for cp in sends:
        cp.wait_send()


def body(queries, cache_pool, page_table, lengths, residual, w_uv, w_out, norm_gain, w_gate, w_down):
    anyspec = pl.BlockSpec(memory_space=pl.ANY)
    smem = pl.BlockSpec(memory_space=pltpu.SMEM)
    vmem = pl.BlockSpec(memory_space=pltpu.VMEM)
    V = pltpu.VMEM
    DMA = pltpu.SemaphoreType.DMA
    return pl.pallas_call(
        kernel,
        out_shape=(jax.ShapeDtypeStruct((8, D), BF), jax.ShapeDtypeStruct((8, D), BF)),
        in_specs=[anyspec, anyspec, smem, smem] + [anyspec] * 6,
        out_specs=(vmem, vmem),
        scratch_shapes=[
            V((8, 64, KW), BF), V((16, 64, KW), BF), V((8, D), BF), V((4, LAT, 128), BF),
            V((2, 512, HALF), BF), V((2, 1, HALF), F32), V((2, HALF, FFL), BF), V((2, FFL, HALF), BF),
            V((4, 512, 128), F32), V((512, LAT), BF), V((Z, 2, 32, LAT), BF), V((4, 128, LAT), BF), V((128, 512), BF),
            V((2, 128, CH), F32), V((2, 2, 128, CH), BF), V((2, 2, 128, CH), BF),
            V((2, NP, 16, CH), BF), V((2, NP, 16, CH), BF),
            V((Z, 2, 16, CH), BF), V((Z, 2, 16, CH), BF), V((2, 128, HALF), BF), V((128, 128), F32), V((128, FFL), BF),
            V((8, HALF), F32), V((2, 8, HALF), F32), V((16, HALF), F32), V((16, HALF), F32), V((8, HALF), F32),
            V((2, 8, HALF), F32), V((2, 8, HALF), F32),
            DMA((12,)), DMA((Z, 2)), DMA((Z, 2)), DMA((2, 2)), DMA((2, 2)), DMA((2, NP)), DMA((2, NP)),
            DMA((NP,)), DMA((NP,)), DMA((Z, 2)), DMA((Z, 2)), DMA((3,)), DMA((3,)),
        ],
        compiler_params=pltpu.CompilerParams(
            collective_id=0, has_side_effects=True, vmem_limit_bytes=48 * 1024 * 1024
        ),
        cost_estimate=pl.CostEstimate(flops=1800000000, bytes_accessed=14400000, transcendentals=100000),
    )(queries, cache_pool, page_table, lengths, residual, w_uv, w_out, norm_gain.reshape(1, D), w_gate, w_down)


def solution(mesh):
    return jax.shard_map(
        body,
        mesh=mesh,
        in_specs=(
            P(("grp", "rank"), None, None),
            P(("grp", "rank"), None, None),
            P(("grp", "rank"), None),
            P(("grp", "rank")),
            P(("grp", "rank"), None),
            P("rank", None, None),
            P("rank", None),
            P(),
            P(None, "rank"),
            P("rank", None),
        ),
        out_specs=(P(("grp", "rank"), None), P(("grp", "rank"), None)),
        check_vma=False,
    )
```

time: 191 us -> 81.6 us (0.43); the launches traced: 188 us -> 81.4 us
  waiting for transfers between devices: 105 us -> 0 us
  Pallas kernels: 0 us -> 71.2 us
  blocking collectives: 47.7 us -> 0 us
  matrix products: 14.6 us -> 0 us
  between operations: 14.1 us -> 0.7 us
  local copies, waits for them, and re-layouts: 2.31 us -> 9.41 us
  other arithmetic: 4.38 us -> 0 us
    reduce_scatter x2 -> x0, waiting for transfers between devices: 105 us -> none  [the longest x1 52.7 us: body(): lax.psum_scatter(partial_value.astype(jnp.bfloat16), 'rank', scatter_dime...]
    pallas_call x0 -> x1, Pallas kernels: none -> 71.2 us  [body(): pl.pallas_call(kernel, out_shape=(jax.ShapeDtypeStruct((8, D), BF), jax.S...]
    all_to_all x1 -> x0, blocking collectives: 27.1 us -> none  [body(): lax.all_to_all(context, 'rank', split_axis=1, concat_axis=0, tiled=True)]
    all_gather x1 -> x0, blocking collectives: 20.6 us -> none  [body(): gathered = lax.all_gather(normed, 'rank', axis=0, tiled=True)]
    dot_general x5 -> x0, matrix products: 14.6 us -> none  [the longest x1 7.79 us: body(): partial_value = jnp.dot(hidden, w_down, preferred_element_type=jnp.float32)]
    unnamed x12 -> x14, local copies, waits for them, and re-layouts: 0.03 us -> 8.69 us
  transfers between devices with their start and end apart: 2 -> 0, of which waited for: 2 -> 0; matrix products, arithmetic and copies ran while one was open for 0% -> 0% of each run, Pallas kernels for 0% -> 0%
where the time goes in v1:
time: 81.6 us; the launch traced here: 81.4 us
  Pallas kernels  71.2 us (87%)
  local copies, waits for them, and re-layouts  9.41 us (12%)
    pallas_call x1, Pallas kernels, body(): pl.pallas_call(kernel, out_shape=(jax.ShapeDtypeStruct((8, D), BF), jax.S...  71.2 us
    unnamed x14, local copies, waits for them, and re-layouts  8.69 us

profile of v1, /device:TPU:1, one launch (start us, length us, event | category | flops | bytes accessed | tf_op | source)
XLA Modules:
  0.0 81.4 jit_solution(15582363646695982788)
XLA Ops:
  0.6 0.8 copy.12.pt
  1.4 0.7 reshape.7.gain_h
  2.1 0.0 copy-start
  2.1 0.0 copy-start.1
  2.1 0.0 copy-start.2
  2.2 0.0 copy-start.3
  2.2 0.0 copy-start.4
  2.2 6.7 %copy.13.wg_h = bf16[3584,576]{1,0:T(8,128)(2,1)} copy(bf16[3584,576]{0,1:T(8,128)(2,1)} %param.18) | data formatting | bytes 8257536 | tf_op args[8]
  8.8 0.0 copy-done
  8.8 0.0 copy-done.1
  8.8 0.0 copy-done.2
  8.8 0.0 copy-done.3
  8.8 0.0 copy-done.4
  8.9 71.2 %shard_map.113 = (bf16[8,3584]{1,0:T(8,128)(2,1)S(1)}, bf16[8,3584]{1,0:T(8,128)(2,1)S(1)}) custom-call(bf16[8,64,576]{2,1,0:T(8,128)(2,1)S(1)} %copy-done.1, bf16[16,64,576]{2,1,0:T(8,128)(2,1)S(1)} %copy-done, s32[8,2]{1,0:T(8,128)S(1)} %copy.12.pt, s32[8]{0:T(128)S(1)} %copy-done.4, bf16[8,3584]{1,0:T(8,128)(2,1)S(1)} %copy-done.3, ...), custom_call_target="tpu_custom_call" | custom-call | flops 1800000000 | bytes 14400000 | tf_op jit(solution)/shard_map/pallas_call | solution.py:282
  80.1 0.6 copy.16
  80.7 0.6 copy.17
Async XLA Ops:
  2.1 6.7 %copy-start = (bf16[16,64,576]{2,1,0:T(8,128)(2,1)S(1)}, bf16[16,64,576]{2,1,0:T(8,128)(2,1)}, u32[]{:S(2)}) copy-start(bf16[16,64,576]{2,1,0:T(8,128)(2,1)} %pool_h.1) | copy-start | bytes 3538948
  2.1 6.7 %copy-start.1 = (bf16[8,64,576]{2,1,0:T(8,128)(2,1)S(1)}, bf16[8,64,576]{2,1,0:T(8,128)(2,1)}, u32[]{:S(2)}) copy-start(bf16[8,64,576]{2,1,0:T(8,128)(2,1)} %q_h.1) | copy-start | bytes 1769476
  2.1 6.7 %copy-start.2 = (bf16[4,512,128]{2,1,0:T(8,128)(2,1)S(1)}, bf16[4,512,128]{2,1,0:T(8,128)(2,1)}, u32[]{:S(2)}) copy-start(bf16[4,512,128]{2,1,0:T(8,128)(2,1)} %wuv_h.1) | copy-start | bytes 1572868
  2.2 6.7 %copy-start.3 = (bf16[8,3584]{1,0:T(8,128)(2,1)S(1)}, bf16[8,3584]{1,0:T(8,128)(2,1)}, u32[]{:S(2)}) copy-start(bf16[8,3584]{1,0:T(8,128)(2,1)} %res_h.1) | copy-start | bytes 172036
  2.2 6.7 %copy-start.4 = (s32[8]{0:T(128)S(1)}, s32[8]{0:T(128)}, u32[]{:S(2)}) copy-start(s32[8]{0:T(128)} %ln.1) | copy-start | bytes 100

commit v2 on v0

v2 whole, which is shorter than its diff:
```python
import jax
import jax.numpy as jnp
from jax import lax
from jax.experimental import pallas as pl
from jax.experimental.pallas import tpu as pltpu
from jax.sharding import PartitionSpec as P

SCALE = 0.07216878364870322
LAT = 512
KW = 576
D = 3584
HALF = 1792
CH = 896
FFL = 576
Z = 8
NB = 2
BF = jnp.bfloat16
F32 = jnp.float32
NT = (((1,), (1,)), ((), ()))
MESH = pl.DeviceIdType.MESH
FAR = (4, 3, 5, 2, 6, 1, 7)


def kernel(
    q_h, pool_h, pt, ln, res_h, wuv_h, wout_h, gain_h, wg_h, wd_h,
    att_o, ffn_o,
    qv, poolv, resv, wuvv, woutv, gain1, gain2, gainv, wgv, wdv,
    ctxa, ctxb, rctx, lhs, vals,
    part, pss, psr, rsb, rrb, gown, goth, xin, sq, hid, res_s, res_r, att, fin, outx_r,
    lsem, a2a_s, a2a_r, ps_ss, ps_rs, rg_ss, rg_rs, ag_ss, ag_rs, sb_ss, sb_rs, ex_ss, ex_rs,
):
    me = lax.axis_index("rank")
    z = lax.div(me, 2)
    c = lax.rem(me, 2)
    sib = me + 1 - 2 * c
    other = {"rank": sib}

    def chip(j):
        return lax.rem(z + j, Z)

    own_col = pl.multiple_of(c * HALF, 128)
    oth_col = pl.multiple_of((1 - c) * HALF, 128)

    copies = []
    sends = []

    def load(src, dst):
        cp = pltpu.make_async_copy(src, dst, lsem.at[len(copies)])
        copies.append(cp)
        cp.start()
        return cp

    l_q = [load(q_h.at[pl.ds(4 * i, 4)], qv.at[pl.ds(4 * i, 4)]) for i in range(NB)]
    l_pool = load(pool_h, poolv)
    l_res = load(res_h, resv)
    l_gain = load(gain_h, gain1)
    l_wuv = load(wuv_h, wuvv)
    l_wout = [load(wout_h.at[:, pl.ds(o, HALF)], woutv.at[i]) for i, o in enumerate((oth_col, own_col))]
    l_wg = [load(wg_h.at[:, pl.ds(o, HALF)], wgv.at[i]) for i, o in enumerate((oth_col, own_col))]
    l_wd = [load(wd_h.at[:, pl.ds(o, HALF)], wdv.at[i]) for i, o in enumerate((oth_col, own_col))]

    barrier = pltpu.get_barrier_semaphore()
    for k in range(1, 16):
        pl.semaphore_signal(barrier, inc=1, device_id={"rank": lax.rem(me + k, 16)}, device_id_type=MESH)

    def remote(src, dst, ss, rs, dev):
        cp = pltpu.make_async_remote_copy(
            src_ref=src, dst_ref=dst, send_sem=ss, recv_sem=rs, device_id=dev, device_id_type=MESH
        )
        cp.start()
        sends.append(cp)

    def arrived(dst, rs):
        pltpu.make_async_copy(dst, dst, rs).wait()

    ri = lax.broadcasted_iota(jnp.int32, (256, 256), 0)
    ci = lax.broadcasted_iota(jnp.int32, (256, 256), 1)
    to_rank = (ci == ((ri >> 2) & 3) * 64 + (ri >> 4) * 4 + (ri & 3)).astype(F32).astype(BF)
    to_head = (ci == (ri & 63) * 4 + (ri >> 6)).astype(F32).astype(BF)
    col = lax.broadcasted_iota(jnp.int32, (64, 128), 1)

    def attend(i):
        for r in range(4):
            b = 4 * i + r
            key = jnp.concatenate([poolv[pt[0, b]], poolv[pt[1, b]]], axis=0)
            s = lax.dot_general(qv[b], key, NT, preferred_element_type=F32) * SCALE
            s = jnp.where(col < ln[b], s, F32(-1e30))
            p = jnp.exp(s - jnp.max(s, axis=-1, keepdims=True))
            w = (p / jnp.sum(p, axis=-1, keepdims=True)).astype(BF)
            ctxa[i, pl.ds(r * 64, 64), :] = jnp.dot(w, key[:, :LAT], preferred_element_type=F32).astype(BF)
        ctxb[i] = jnp.dot(to_rank, ctxa[i], preferred_element_type=F32).astype(BF)

    def send_contexts(i):
        def block(rank):
            return pl.ds(pl.multiple_of(rank * 16, 16), 16)

        for j in FAR:
            for k in (0, 1):
                dst = chip(j) * 2 + k
                remote(
                    ctxb.at[i, block(dst), :], rctx.at[i, 8 - j, c], a2a_s.at[i, j, k], a2a_r.at[i, 8 - j, c], {"rank": dst}
                )
        remote(ctxb.at[i, block(sib), :], rctx.at[i, 0, c], a2a_s.at[i, 0, 0], a2a_r.at[i, 0, c], other)
        rctx[i, 0, c] = ctxb[i, block(me), :]

    def project(i):
        arrived(rctx.at[i, 0, 1 - c], a2a_r.at[i, 0, 1 - c])
        for j in FAR:
            for k in (0, 1):
                arrived(rctx.at[i, j, k], a2a_r.at[i, j, k])
        lhs[i] = jnp.dot(to_head, rctx[i].reshape(256, LAT), preferred_element_type=F32).astype(BF)
        for h in range(4):
            v = jnp.dot(lhs[i, pl.ds(h * 64, 64), :], wuvv[h], preferred_element_type=F32)
            vals[i, :, pl.ds(h * 128, 128)] = v.astype(BF)

    def pair_start(t, i, left, weights):
        for k in (0, 1):
            o = jnp.dot(left, weights[0, :, pl.ds(k * CH, CH)], preferred_element_type=F32)
            pss[t, i, k] = o.astype(BF)
            remote(pss.at[t, i, k], psr.at[t, i, k], ps_ss.at[t, i, k], ps_rs.at[t, i, k], other)
        for k in (0, 1):
            part[t, i, k] = jnp.dot(left, weights[1, :, pl.ds(k * CH, CH)], preferred_element_type=F32)

    def scatter_start(t, i):
        for k in (0, 1):
            arrived(psr.at[t, i, k], ps_rs.at[t, i, k])
            part[t, i, k] = part[t, i, k] + psr[t, i, k].astype(F32)
        for j in FAR:
            rows = pl.ds(8 * j, 8)
            rsb[t, i, j] = jnp.concatenate([part[t, i, 0, rows, :], part[t, i, 1, rows, :]], axis=0).astype(BF)
            remote(
                rsb.at[t, i, j], rrb.at[t, i, 8 - j], rg_ss.at[t, i, j], rg_rs.at[t, i, 8 - j], {"rank": chip(j) * 2 + c}
            )

    def scatter_end(t, i):
        acc = jnp.concatenate([part[t, i, 0, pl.ds(0, 8), :], part[t, i, 1, pl.ds(0, 8), :]], axis=0)
        for j in FAR:
            arrived(rrb.at[t, i, j], rg_rs.at[t, i, j])
            acc = acc + rrb[t, i, j].astype(F32)
        return acc

    def prepare(i, src, half, slot):
        rows = pl.ds(slot * 8, 8)
        v = src.astype(F32)
        tot = jnp.zeros((8, 128), F32)
        for k in (0, 1):
            u = v[8 * k : 8 * k + 8]
            xin[i, half, rows, pl.ds(k * CH, CH)] = u * gainv[half, :, pl.ds(k * CH, CH)]
            u = u * u
            for n in range(CH // 128):
                tot = tot + u[:, n * 128 : (n + 1) * 128]
        sq[i, half, rows, :] = tot

    def gather_start(i, attn):
        res = jnp.concatenate(
            [res_r[c2, 4 * i : 4 * i + 4, k * CH : (k + 1) * CH] for k in (0, 1) for c2 in (0, 1)], axis=0
        )
        a = (attn + res).astype(BF)
        gown[i, 0] = a
        for j in FAR:
            remote(gown.at[i, 0], gown.at[i, 8 - j], ag_ss.at[i, j], ag_rs.at[i, 8 - j], {"rank": chip(j) * 2 + c})
        remote(gown.at[i, 0], goth.at[i, 0], sb_ss.at[i, 0], sb_rs.at[i, 0], other)
        att[0, i] = a.astype(F32)
        remote(att.at[0, i], outx_r.at[0, i], ex_ss.at[1, i], ex_rs.at[1, i], other)
        prepare(i, a, 1, 0)

    def gather_end(i):
        for j in FAR:
            arrived(gown.at[i, j], ag_rs.at[i, j])
            remote(gown.at[i, j], goth.at[i, j], sb_ss.at[i, j], sb_rs.at[i, j], other)
            prepare(i, gown[i, j], 1, j)
        acc = lax.dot_general(xin[i, 1].astype(BF), wgv[1], NT, preferred_element_type=F32)
        for j in (0,) + FAR:
            arrived(goth.at[i, j], sb_rs.at[i, j])
            prepare(i, goth[i, j], 0, j)
        acc = acc + lax.dot_general(xin[i, 0].astype(BF), wgv[0], NT, preferred_element_type=F32)
        ms = jnp.sum(sq[i, 0] + sq[i, 1], axis=-1, keepdims=True) * F32(1.0 / D)
        g = acc * lax.rsqrt(ms + F32(1e-6))
        hid[i] = (g / (1.0 + jnp.exp(-g))).astype(BF)

    l_pool.wait()
    for i in range(NB):
        l_q[i].wait()
        attend(i)
        if i == 0:
            pl.semaphore_wait(barrier, 15)
        send_contexts(i)

    l_res.wait()
    res_r[c] = resv[:, pl.ds(own_col, HALF)].astype(F32)
    res_s[...] = resv[:, pl.ds(oth_col, HALF)].astype(F32)
    remote(res_s, res_r.at[c], ex_ss.at[0, 0], ex_rs.at[0, 0], other)
    l_gain.wait()
    gain2[...] = gain1[...].reshape(1, D)
    gainv[0] = gain2[:, pl.ds(oth_col, HALF)]
    gainv[1] = gain2[:, pl.ds(own_col, HALF)]

    l_wuv.wait()
    for w in l_wout:
        w.wait()
    for i in range(NB):
        project(i)
        pair_start(0, i, vals[i], woutv)
        scatter_start(0, i)
    arrived(res_r.at[1 - c], ex_rs.at[0, 0])
    for i in range(NB):
        gather_start(i, scatter_end(0, i))
    for w in l_wg + l_wd:
        w.wait()
    for i in range(NB):
        gather_end(i)
        pair_start(1, i, hid[i], wdv)
        scatter_start(1, i)
    for i in range(NB):
        fin[i] = (att[0, i] + scatter_end(1, i)).astype(BF).astype(F32)
        remote(fin.at[i], outx_r.at[1, i], ex_ss.at[2, i], ex_rs.at[2, i], other)

    def rows_of(blocks, k):
        parts = []
        for i in range(NB):
            v = blocks[i]
            parts.append(jnp.where(c == 0, v[8 * k : 8 * k + 4], v[8 * k + 4 : 8 * k + 8]))
        return jnp.concatenate(parts, axis=0).astype(BF)

    for k in (0, 1):
        att_o[:, pl.ds(pl.multiple_of(own_col + k * CH, 128), CH)] = rows_of([att[0, i] for i in range(NB)], k)
        ffn_o[:, pl.ds(pl.multiple_of(own_col + k * CH, 128), CH)] = rows_of([fin[i] for i in range(NB)], k)
    for t, o in ((0, att_o), (1, ffn_o)):
        for i in range(NB):
            arrived(outx_r.at[t, i], ex_rs.at[t + 1, i])
        for k in (0, 1):
            o[:, pl.ds(pl.multiple_of(oth_col + k * CH, 128), CH)] = rows_of([outx_r[t, i] for i in range(NB)], k)
    for cp in sends:
        cp.wait_send()


def body(queries, cache_pool, page_table, lengths, residual, w_uv, w_out, norm_gain, w_gate, w_down):
    anyspec = pl.BlockSpec(memory_space=pl.ANY)
    smem = pl.BlockSpec(memory_space=pltpu.SMEM)
    vmem = pl.BlockSpec(memory_space=pltpu.VMEM)
    V = pltpu.VMEM
    DMA = pltpu.SemaphoreType.DMA
    return pl.pallas_call(
        kernel,
        out_shape=(jax.ShapeDtypeStruct((8, D), BF), jax.ShapeDtypeStruct((8, D), BF)),
        in_specs=[anyspec, anyspec, smem, smem] + [anyspec] * 6,
        out_specs=(vmem, vmem),
        scratch_shapes=[
            V((8, 64, KW), BF), V((16, 64, KW), BF), V((8, D), BF), V((4, LAT, 128), BF),
            V((2, 512, HALF), BF), V((D,), F32), V((1, D), F32), V((2, 1, HALF), F32), V((2, FFL, HALF), BF), V((2, FFL, HALF), BF),
            V((NB, 256, LAT), BF), V((NB, 256, LAT), BF), V((NB, Z, 2, 16, LAT), BF), V((NB, 256, LAT), BF), V((NB, 64, 512), BF),
            V((2, NB, 2, 64, CH), F32), V((2, NB, 2, 64, CH), BF), V((2, NB, 2, 64, CH), BF),
            V((2, NB, Z, 16, CH), BF), V((2, NB, Z, 16, CH), BF),
            V((NB, Z, 16, CH), BF), V((NB, Z, 16, CH), BF), V((NB, 2, 64, HALF), F32), V((NB, 2, 64, 128), F32), V((NB, 64, FFL), BF),
            V((8, HALF), F32), V((2, 8, HALF), F32), V((1, NB, 16, CH), F32), V((NB, 16, CH), F32), V((2, NB, 16, CH), F32),
            DMA((16,)), DMA((NB, Z, 2)), DMA((NB, Z, 2)), DMA((2, NB, 2)), DMA((2, NB, 2)), DMA((2, NB, Z)), DMA((2, NB, Z)),
            DMA((NB, Z)), DMA((NB, Z)), DMA((NB, Z)), DMA((NB, Z)), DMA((3, NB)), DMA((3, NB)),
        ],
        compiler_params=pltpu.CompilerParams(
            collective_id=0, has_side_effects=True, vmem_limit_bytes=60 * 1024 * 1024
        ),
        cost_estimate=pl.CostEstimate(flops=1800000000, bytes_accessed=14400000, transcendentals=100000),
    )(queries, cache_pool, page_table.T, lengths, residual, w_uv, w_out, norm_gain, w_gate.T, w_down)


def solution(mesh):
    return jax.shard_map(
        body,
        mesh=mesh,
        in_specs=(
            P(("grp", "rank"), None, None),
            P(("grp", "rank"), None, None),
            P(("grp", "rank"), None),
            P(("grp", "rank")),
            P(("grp", "rank"), None),
            P("rank", None, None),
            P("rank", None),
            P(),
            P(None, "rank"),
            P("rank", None),
        ),
        out_specs=(P(("grp", "rank"), None), P(("grp", "rank"), None)),
        check_vma=False,
    )
```

time: 191 us -> 62.2 us (0.33); the launches traced: 188 us -> 62 us
  waiting for transfers between devices: 105 us -> 0 us
  Pallas kernels: 0 us -> 58.5 us
  blocking collectives: 47.7 us -> 0 us
  matrix products: 14.6 us -> 0 us
  between operations: 14.1 us -> 0.64 us
  other arithmetic: 4.38 us -> 0 us
    reduce_scatter x2 -> x0, waiting for transfers between devices: 105 us -> none  [the longest x1 52.7 us: body(): lax.psum_scatter(partial_value.astype(jnp.bfloat16), 'rank', scatter_dime...]
    pallas_call x0 -> x1, Pallas kernels: none -> 58.5 us  [body(): pl.pallas_call(kernel, out_shape=(jax.ShapeDtypeStruct((8, D), BF), jax.S...]
    all_to_all x1 -> x0, blocking collectives: 27.1 us -> none  [body(): lax.all_to_all(context, 'rank', split_axis=1, concat_axis=0, tiled=True)]
    all_gather x1 -> x0, blocking collectives: 20.6 us -> none  [body(): gathered = lax.all_gather(normed, 'rank', axis=0, tiled=True)]
    dot_general x5 -> x0, matrix products: 14.6 us -> none  [the longest x1 7.79 us: body(): partial_value = jnp.dot(hidden, w_down, preferred_element_type=jnp.float32)]
    unnamed x12 -> x2, local copies, waits for them, and re-layouts: 0.03 us -> 2.89 us
  transfers between devices with their start and end apart: 2 -> 0, of which waited for: 2 -> 0; matrix products, arithmetic and copies ran while one was open for 0% -> 0% of each run, Pallas kernels for 0% -> 0%
where the time goes in v2:
time: 62.2 us; the launch traced here: 62 us
  Pallas kernels  58.5 us (94%)
  local copies, waits for them, and re-layouts  2.89 us (5%)
  between operations  0.64 us (1%)
    pallas_call x1, Pallas kernels, body(): pl.pallas_call(kernel, out_shape=(jax.ShapeDtypeStruct((8, D), BF), jax.S...  58.5 us
    unnamed x2, local copies, waits for them, and re-layouts  2.89 us

profile of v2, /device:TPU:1, one launch (start us, length us, event | category | flops | bytes accessed | tf_op | source)
XLA Modules:
  0.0 62.0 jit_solution(6854082921337141448)
XLA Ops:
  0.6 58.5 %shard_map.113 = (bf16[8,3584]{1,0:T(8,128)(2,1)}, bf16[8,3584]{1,0:T(8,128)(2,1)}) custom-call(bf16[8,64,576]{2,1,0:T(8,128)(2,1)} %q_h.1, bf16[16,64,576]{2,1,0:T(8,128)(2,1)} %pool_h.1, s32[2,8]{1,0:T(2,128)} %bitcast.3, s32[8]{0:T(128)} %ln.1, bf16[8,3584]{1,0:T(8,128)(2,1)} %res_h.1, bf16[4,512,128]{2,1,0:T(8,128)(2,1)} %wuv_h.1, ...), custom_call_target="tpu_custom_call" | custom-call | flops 1800000000 | bytes 14400000 | tf_op jit(solution)/shard_map/pallas_call | solution.py:243
  59.1 1.4 %copy.14 = bf16[8,3584]{1,0:T(8,128)(2,1)} copy(bf16[8,3584]{1,0:T(8,128)(2,1)} %get-tuple-element.4) | data formatting | bytes 114688
  60.6 1.4 %copy.15 = bf16[8,3584]{1,0:T(8,128)(2,1)} copy(bf16[8,3584]{1,0:T(8,128)(2,1)} %get-tuple-element.5) | data formatting | bytes 114688

commit v3 on v2

--- a/solution.py
+++ b/solution.py
@@ -26,8 +26,8 @@
     att_o, ffn_o,
     qv, poolv, resv, wuvv, woutv, gain1, gain2, gainv, wgv, wdv,
     ctxa, ctxb, rctx, lhs, vals,
-    part, pss, psr, rsb, rrb, gown, goth, xin, sq, hid, res_s, res_r, att, fin, outx_r,
-    lsem, a2a_s, a2a_r, ps_ss, ps_rs, rg_ss, rg_rs, ag_ss, ag_rs, sb_ss, sb_rs, ex_ss, ex_rs,
+    part, rsb, rrb, gown, xin, sq, pre, hid, res_s, res_r, att, fin, outx_r,
+    lsem, a2a_s, a2a_r, w_ss, w_rs, v_ss, v_rs, rg_ss, rg_rs, ag_ss, ag_rs, h_ss, h_rs, ex_ss, ex_rs,
 ):
     me = lax.axis_index("rank")
     z = lax.div(me, 2)
@@ -41,6 +41,10 @@
     own_col = pl.multiple_of(c * HALF, 128)
     oth_col = pl.multiple_of((1 - c) * HALF, 128)
 
+    barrier = pltpu.get_barrier_semaphore()
+    for k in (8, 9, 7, 6, 10, 5, 11, 4, 12, 3, 13, 2, 14, 1, 15):
+        pl.semaphore_signal(barrier, inc=1, device_id={"rank": lax.rem(me + k, 16)}, device_id_type=MESH)
+
     copies = []
     sends = []
 
@@ -55,13 +59,9 @@
     l_res = load(res_h, resv)
     l_gain = load(gain_h, gain1)
     l_wuv = load(wuv_h, wuvv)
-    l_wout = [load(wout_h.at[:, pl.ds(o, HALF)], woutv.at[i]) for i, o in enumerate((oth_col, own_col))]
-    l_wg = [load(wg_h.at[:, pl.ds(o, HALF)], wgv.at[i]) for i, o in enumerate((oth_col, own_col))]
-    l_wd = [load(wd_h.at[:, pl.ds(o, HALF)], wdv.at[i]) for i, o in enumerate((oth_col, own_col))]
-
-    barrier = pltpu.get_barrier_semaphore()
-    for k in range(1, 16):
-        pl.semaphore_signal(barrier, inc=1, device_id={"rank": lax.rem(me + k, 16)}, device_id_type=MESH)
+    l_wout = load(wout_h.at[:, pl.ds(own_col, HALF)], woutv.at[0])
+    l_wg = load(wg_h.at[:, pl.ds(own_col, HALF)], wgv.at[0])
+    l_wd = load(wd_h.at[:, pl.ds(own_col, HALF)], wdv.at[0])
 
     def remote(src, dst, ss, rs, dev):
         cp = pltpu.make_async_remote_copy(
@@ -111,20 +111,19 @@
         lhs[i] = jnp.dot(to_head, rctx[i].reshape(256, LAT), preferred_element_type=F32).astype(BF)
         for h in range(4):
             v = jnp.dot(lhs[i, pl.ds(h * 64, 64), :], wuvv[h], preferred_element_type=F32)
-            vals[i, :, pl.ds(h * 128, 128)] = v.astype(BF)
-
-    def pair_start(t, i, left, weights):
+            vals[i, 0, :, pl.ds(h * 128, 128)] = v.astype(BF)
+        remote(vals.at[i, 0], vals.at[i, 1], v_ss.at[i], v_rs.at[i], other)
+
+    def multiply(t, i, left, weights, ready):
         for k in (0, 1):
-            o = jnp.dot(left, weights[0, :, pl.ds(k * CH, CH)], preferred_element_type=F32)
-            pss[t, i, k] = o.astype(BF)
-            remote(pss.at[t, i, k], psr.at[t, i, k], ps_ss.at[t, i, k], ps_rs.at[t, i, k], other)
+            part[t, i, k] = jnp.dot(left[i, 0], weights[0, :, pl.ds(k * CH, CH)], preferred_element_type=F32)
+        if ready:
+            arrived(left.at[i, 1], v_rs.at[i])
         for k in (0, 1):
-            part[t, i, k] = jnp.dot(left, weights[1, :, pl.ds(k * CH, CH)], preferred_element_type=F32)
+            o = jnp.dot(left[i, 1], weights[1, :, pl.ds(k * CH, CH)], preferred_element_type=F32)
+            part[t, i, k] = part[t, i, k] + o
 
     def scatter_start(t, i):
-        for k in (0, 1):
-            arrived(psr.at[t, i, k], ps_rs.at[t, i, k])
-            part[t, i, k] = part[t, i, k] + psr[t, i, k].astype(F32)
         for j in FAR:
             rows = pl.ds(8 * j, 8)
             rsb[t, i, j] = jnp.concatenate([part[t, i, 0, rows, :], part[t, i, 1, rows, :]], axis=0).astype(BF)
@@ -139,17 +138,17 @@
             acc = acc + rrb[t, i, j].astype(F32)
         return acc
 
-    def prepare(i, src, half, slot):
+    def prepare(i, src, slot):
         rows = pl.ds(slot * 8, 8)
         v = src.astype(F32)
         tot = jnp.zeros((8, 128), F32)
         for k in (0, 1):
             u = v[8 * k : 8 * k + 8]
-            xin[i, half, rows, pl.ds(k * CH, CH)] = u * gainv[half, :, pl.ds(k * CH, CH)]
+            xin[i, rows, pl.ds(k * CH, CH)] = u * gainv[:, pl.ds(k * CH, CH)]
             u = u * u
             for n in range(CH // 128):
                 tot = tot + u[:, n * 128 : (n + 1) * 128]
-        sq[i, half, rows, :] = tot
+        sq[i, 0, rows, :] = tot
 
     def gather_start(i, attn):
         res = jnp.concatenate(
@@ -159,32 +158,43 @@
         gown[i, 0] = a
         for j in FAR:
             remote(gown.at[i, 0], gown.at[i, 8 - j], ag_ss.at[i, j], ag_rs.at[i, 8 - j], {"rank": chip(j) * 2 + c})
-        remote(gown.at[i, 0], goth.at[i, 0], sb_ss.at[i, 0], sb_rs.at[i, 0], other)
         att[0, i] = a.astype(F32)
         remote(att.at[0, i], outx_r.at[0, i], ex_ss.at[1, i], ex_rs.at[1, i], other)
-        prepare(i, a, 1, 0)
+        prepare(i, a, 0)
 
     def gather_end(i):
         for j in FAR:
             arrived(gown.at[i, j], ag_rs.at[i, j])
-            remote(gown.at[i, j], goth.at[i, j], sb_ss.at[i, j], sb_rs.at[i, j], other)
-            prepare(i, gown[i, j], 1, j)
-        acc = lax.dot_general(xin[i, 1].astype(BF), wgv[1], NT, preferred_element_type=F32)
-        for j in (0,) + FAR:
-            arrived(goth.at[i, j], sb_rs.at[i, j])
-            prepare(i, goth[i, j], 0, j)
-        acc = acc + lax.dot_general(xin[i, 0].astype(BF), wgv[0], NT, preferred_element_type=F32)
+            prepare(i, gown[i, j], j)
+        remote(sq.at[i, 0], sq.at[i, 1], h_ss.at[i, 2], h_rs.at[i, 2], other)
+        x = xin[i].astype(BF)
+        for u in (1, 0):
+            pre[i, 0, u] = lax.dot_general(x, wgv[u], NT, preferred_element_type=F32).astype(BF)
+            remote(pre.at[i, 0, u], pre.at[i, 1, 1 - u], h_ss.at[i, u], h_rs.at[i, 1 - u], other)
+
+    def activate(i):
+        arrived(sq.at[i, 1], h_rs.at[i, 2])
         ms = jnp.sum(sq[i, 0] + sq[i, 1], axis=-1, keepdims=True) * F32(1.0 / D)
-        g = acc * lax.rsqrt(ms + F32(1e-6))
-        hid[i] = (g / (1.0 + jnp.exp(-g))).astype(BF)
+        inv = lax.rsqrt(ms + F32(1e-6))
+        for u in (0, 1):
+            arrived(pre.at[i, 1, u], h_rs.at[i, u])
+            g = (pre[i, 0, u].astype(F32) + pre[i, 1, u].astype(F32)) * inv
+            hid[i, u] = (g / (1.0 + jnp.exp(-g))).astype(BF)
+
+    def push(src, dst, n):
+        remote(src.at[:, pl.ds(oth_col, HALF)], dst.at[1], w_ss.at[n], w_rs.at[n], other)
 
     l_pool.wait()
-    for i in range(NB):
-        l_q[i].wait()
-        attend(i)
-        if i == 0:
-            pl.semaphore_wait(barrier, 15)
-        send_contexts(i)
+    l_q[0].wait()
+    attend(0)
+    pl.semaphore_wait(barrier, 15)
+    push(wout_h, woutv, 0)
+    push(wg_h, wgv, 1)
+    push(wd_h, wdv, 2)
+    send_contexts(0)
+    l_q[1].wait()
+    attend(1)
+    send_contexts(1)
 
     l_res.wait()
     res_r[c] = resv[:, pl.ds(own_col, HALF)].astype(F32)
@@ -192,28 +202,34 @@
     remote(res_s, res_r.at[c], ex_ss.at[0, 0], ex_rs.at[0, 0], other)
     l_gain.wait()
     gain2[...] = gain1[...].reshape(1, D)
-    gainv[0] = gain2[:, pl.ds(oth_col, HALF)]
-    gainv[1] = gain2[:, pl.ds(own_col, HALF)]
+    gainv[...] = gain2[:, pl.ds(own_col, HALF)]
 
     l_wuv.wait()
-    for w in l_wout:
-        w.wait()
+    l_wout.wait()
+    arrived(woutv.at[1], w_rs.at[0])
+
+    def finish(i):
+        fin[i] = (att[0, i] + scatter_end(1, i)).astype(BF).astype(F32)
+        remote(fin.at[i], outx_r.at[1, i], ex_ss.at[2, i], ex_rs.at[2, i], other)
+
     for i in range(NB):
         project(i)
-        pair_start(0, i, vals[i], woutv)
+        multiply(0, i, vals, woutv, True)
         scatter_start(0, i)
     arrived(res_r.at[1 - c], ex_rs.at[0, 0])
     for i in range(NB):
         gather_start(i, scatter_end(0, i))
-    for w in l_wg + l_wd:
-        w.wait()
+    l_wg.wait()
+    arrived(wgv.at[1], w_rs.at[1])
+    l_wd.wait()
+    arrived(wdv.at[1], w_rs.at[2])
     for i in range(NB):
         gather_end(i)
-        pair_start(1, i, hid[i], wdv)
+        activate(i)
+        multiply(1, i, hid, wdv, False)
         scatter_start(1, i)
     for i in range(NB):
-        fin[i] = (att[0, i] + scatter_end(1, i)).astype(BF).astype(F32)
-        remote(fin.at[i], outx_r.at[1, i], ex_ss.at[2, i], ex_rs.at[2, i], other)
+        finish(i)
 
     def rows_of(blocks, k):
         parts = []
@@ -234,33 +250,43 @@
         cp.wait_send()
 
 
+def keep(a, b, att_o, ffn_o):
+    att_o[...] = a[...]
+    ffn_o[...] = b[...]
+
+
 def body(queries, cache_pool, page_table, lengths, residual, w_uv, w_out, norm_gain, w_gate, w_down):
     anyspec = pl.BlockSpec(memory_space=pl.ANY)
     smem = pl.BlockSpec(memory_space=pltpu.SMEM)
     vmem = pl.BlockSpec(memory_space=pltpu.VMEM)
     V = pltpu.VMEM
     DMA = pltpu.SemaphoreType.DMA
-    return pl.pallas_call(
+    att, ffn = pl.pallas_call(
         kernel,
         out_shape=(jax.ShapeDtypeStruct((8, D), BF), jax.ShapeDtypeStruct((8, D), BF)),
         in_specs=[anyspec, anyspec, smem, smem] + [anyspec] * 6,
         out_specs=(vmem, vmem),
         scratch_shapes=[
             V((8, 64, KW), BF), V((16, 64, KW), BF), V((8, D), BF), V((4, LAT, 128), BF),
-            V((2, 512, HALF), BF), V((D,), F32), V((1, D), F32), V((2, 1, HALF), F32), V((2, FFL, HALF), BF), V((2, FFL, HALF), BF),
-            V((NB, 256, LAT), BF), V((NB, 256, LAT), BF), V((NB, Z, 2, 16, LAT), BF), V((NB, 256, LAT), BF), V((NB, 64, 512), BF),
-            V((2, NB, 2, 64, CH), F32), V((2, NB, 2, 64, CH), BF), V((2, NB, 2, 64, CH), BF),
-            V((2, NB, Z, 16, CH), BF), V((2, NB, Z, 16, CH), BF),
-            V((NB, Z, 16, CH), BF), V((NB, Z, 16, CH), BF), V((NB, 2, 64, HALF), F32), V((NB, 2, 64, 128), F32), V((NB, 64, FFL), BF),
+            V((2, 512, HALF), BF), V((D,), F32), V((1, D), F32), V((1, HALF), F32), V((2, FFL, HALF), BF), V((2, FFL, HALF), BF),
+            V((NB, 256, LAT), BF), V((NB, 256, LAT), BF), V((NB, Z, 2, 16, LAT), BF), V((NB, 256, LAT), BF), V((NB, 2, 64, 512), BF),
+            V((2, NB, 2, 64, CH), F32), V((2, NB, Z, 16, CH), BF), V((2, NB, Z, 16, CH), BF),
+            V((NB, Z, 16, CH), BF), V((NB, 64, HALF), F32), V((NB, 2, 64, 128), F32), V((NB, 2, 2, 64, FFL), BF), V((NB, 2, 64, FFL), BF),
             V((8, HALF), F32), V((2, 8, HALF), F32), V((1, NB, 16, CH), F32), V((NB, 16, CH), F32), V((2, NB, 16, CH), F32),
-            DMA((16,)), DMA((NB, Z, 2)), DMA((NB, Z, 2)), DMA((2, NB, 2)), DMA((2, NB, 2)), DMA((2, NB, Z)), DMA((2, NB, Z)),
-            DMA((NB, Z)), DMA((NB, Z)), DMA((NB, Z)), DMA((NB, Z)), DMA((3, NB)), DMA((3, NB)),
+            DMA((16,)), DMA((NB, Z, 2)), DMA((NB, Z, 2)), DMA((3,)), DMA((3,)), DMA((NB,)), DMA((NB,)), DMA((2, NB, Z)), DMA((2, NB, Z)),
+            DMA((NB, Z)), DMA((NB, Z)), DMA((NB, 3)), DMA((NB, 3)), DMA((3, NB)), DMA((3, NB)),
         ],
         compiler_params=pltpu.CompilerParams(
             collective_id=0, has_side_effects=True, vmem_limit_bytes=60 * 1024 * 1024
         ),
         cost_estimate=pl.CostEstimate(flops=1800000000, bytes_accessed=14400000, transcendentals=100000),
     )(queries, cache_pool, page_table.T, lengths, residual, w_uv, w_out, norm_gain, w_gate.T, w_down)
+    return pl.pallas_call(
+        keep,
+        out_shape=(jax.ShapeDtypeStruct((8, D), BF), jax.ShapeDtypeStruct((8, D), BF)),
+        in_specs=[vmem, vmem],
+        out_specs=(vmem, vmem),
+    )(att, ffn)
 
 
 def solution(mesh):

time: 62.2 us -> 59.9 us (0.963)
  local copies, waits for them, and re-layouts: 2.89 us -> 0 us
    unnamed x2 -> x0, local copies, waits for them, and re-layouts: 2.89 us -> none
    pallas_call x0 -> x1, Pallas kernels: none -> 1.49 us  [body(): pl.pallas_call(keep, out_shape=(jax.ShapeDtypeStruct((8, D), BF), jax.Sha...]
    pallas_call x1, Pallas kernels: 58.5 us -> 57.6 us  [body(): pl.pallas_call(kernel, out_shape=(jax.ShapeDtypeStruct((8, D), BF), jax.S...]
where the time goes in v3:
time: 59.9 us; the launch traced here: 59.8 us
  Pallas kernels  59.1 us (99%)
  between operations  0.64 us (1%)
    pallas_call x1, Pallas kernels, body(): pl.pallas_call(kernel, out_shape=(jax.ShapeDtypeStruct((8, D), BF), jax.S...  57.6 us
    pallas_call x1, Pallas kernels, body(): pl.pallas_call(keep, out_shape=(jax.ShapeDtypeStruct((8, D), BF), jax.Sha...  1.49 us

profile of v3, /device:TPU:1, one launch (start us, length us, event | category | flops | bytes accessed | tf_op | source)
XLA Modules:
  0.0 59.8 jit_solution(11742301660443837394)
XLA Ops:
  0.6 57.6 %shard_map.113 = (bf16[8,3584]{1,0:T(8,128)(2,1)}, bf16[8,3584]{1,0:T(8,128)(2,1)}) custom-call(bf16[8,64,576]{2,1,0:T(8,128)(2,1)} %q_h.1, bf16[16,64,576]{2,1,0:T(8,128)(2,1)} %pool_h.1, s32[2,8]{1,0:T(2,128)} %bitcast.3, s32[8]{0:T(128)} %ln.1, bf16[8,3584]{1,0:T(8,128)(2,1)} %res_h.1, bf16[4,512,128]{2,1,0:T(8,128)(2,1)} %wuv_h.1, ...), custom_call_target="tpu_custom_call" | custom-call | flops 1800000000 | bytes 14400000 | tf_op jit(solution)/shard_map/pallas_call | solution.py:264
  58.3 1.5 %shard_map.114 = (bf16[8,3584]{1,0:T(8,128)(2,1)}, bf16[8,3584]{1,0:T(8,128)(2,1)}) custom-call(bf16[8,3584]{1,0:T(8,128)(2,1)} %get-tuple-element.4.a, bf16[8,3584]{1,0:T(8,128)(2,1)} %get-tuple-element.5.b), custom_call_target="tpu_custom_call" | custom-call | tf_op jit(solution)/shard_map/pallas_call | solution.py:284

commit v4 on v3

--- a/solution.py
+++ b/solution.py
@@ -34,6 +34,8 @@
     c = lax.rem(me, 2)
     sib = me + 1 - 2 * c
     other = {"rank": sib}
+    odd = lax.rem(z, 2)
+    two = 2 + 4 * odd
 
     def chip(j):
         return lax.rem(z + j, Z)
@@ -123,17 +125,42 @@
             o = jnp.dot(left[i, 1], weights[1, :, pl.ds(k * CH, CH)], preferred_element_type=F32)
             part[t, i, k] = part[t, i, k] + o
 
+    def scatter_send(t, i, j, slot, dst, extra):
+        rows = pl.ds(8 * j, 8)
+        acc = jnp.concatenate([part[t, i, 0, rows, :], part[t, i, 1, rows, :]], axis=0)
+        for e in extra:
+            acc = acc + e
+        rsb[t, i, j] = acc.astype(BF)
+        remote(
+            rsb.at[t, i, j], rrb.at[t, i, slot], rg_ss.at[t, i, j], rg_rs.at[t, i, slot], {"rank": dst * 2 + c}
+        )
+
+    def relayed(t, i):
+        return t == 0 and i == 1
+
     def scatter_start(t, i):
-        for j in FAR:
-            rows = pl.ds(8 * j, 8)
-            rsb[t, i, j] = jnp.concatenate([part[t, i, 0, rows, :], part[t, i, 1, rows, :]], axis=0).astype(BF)
-            remote(
-                rsb.at[t, i, j], rrb.at[t, i, 8 - j], rg_ss.at[t, i, j], rg_rs.at[t, i, 8 - j], {"rank": chip(j) * 2 + c}
-            )
+        if not relayed(t, i):
+            for j in FAR:
+                scatter_send(t, i, j, 8 - j, chip(j), ())
+        else:
+            scatter_send(t, i, 4, 4, chip(two), ())
+            scatter_send(t, i, 3, 3, chip(1), ())
+            scatter_send(t, i, 5, 5, chip(7), ())
+            scatter_send(t, i, 1, 7, chip(1), ())
+            scatter_send(t, i, 7, 1, chip(7), ())
+
+    def scatter_mid(t, i):
+        arrived(rrb.at[t, i, 4], rg_rs.at[t, i, 4])
+        far = rrb[t, i, 4].astype(F32)
+        none = jnp.zeros_like(far)
+        arrived(rrb.at[t, i, 3], rg_rs.at[t, i, 3])
+        scatter_send(t, i, 2, 6, chip(2), (rrb[t, i, 3].astype(F32), jnp.where(odd == 0, far, none)))
+        arrived(rrb.at[t, i, 5], rg_rs.at[t, i, 5])
+        scatter_send(t, i, 6, 2, chip(6), (rrb[t, i, 5].astype(F32), jnp.where(odd == 0, none, far)))
 
     def scatter_end(t, i):
         acc = jnp.concatenate([part[t, i, 0, pl.ds(0, 8), :], part[t, i, 1, pl.ds(0, 8), :]], axis=0)
-        for j in FAR:
+        for j in (1, 7, 2, 6) if relayed(t, i) else FAR:
             arrived(rrb.at[t, i, j], rg_rs.at[t, i, j])
             acc = acc + rrb[t, i, j].astype(F32)
         return acc
@@ -150,6 +177,9 @@
                 tot = tot + u[:, n * 128 : (n + 1) * 128]
         sq[i, 0, rows, :] = tot
 
+    def gather_send(i, src, slot, dst):
+        remote(gown.at[i, src], gown.at[i, slot], ag_ss.at[i, slot], ag_rs.at[i, slot], {"rank": dst * 2 + c})
+
     def gather_start(i, attn):
         res = jnp.concatenate(
             [res_r[c2, 4 * i : 4 * i + 4, k * CH : (k + 1) * CH] for k in (0, 1) for c2 in (0, 1)], axis=0
@@ -157,7 +187,7 @@
         a = (attn + res).astype(BF)
         gown[i, 0] = a
         for j in FAR:
-            remote(gown.at[i, 0], gown.at[i, 8 - j], ag_ss.at[i, j], ag_rs.at[i, 8 - j], {"rank": chip(j) * 2 + c})
+            gather_send(i, 0, 8 - j, chip(j))
         att[0, i] = a.astype(F32)
         remote(att.at[0, i], outx_r.at[0, i], ex_ss.at[1, i], ex_rs.at[1, i], other)
         prepare(i, a, 0)
@@ -212,24 +242,30 @@
         fin[i] = (att[0, i] + scatter_end(1, i)).astype(BF).astype(F32)
         remote(fin.at[i], outx_r.at[1, i], ex_ss.at[2, i], ex_rs.at[2, i], other)
 
-    for i in range(NB):
-        project(i)
-        multiply(0, i, vals, woutv, True)
-        scatter_start(0, i)
+    project(0)
+    multiply(0, 0, vals, woutv, True)
+    scatter_start(0, 0)
+    project(1)
+    multiply(0, 1, vals, woutv, True)
+    scatter_start(0, 1)
     arrived(res_r.at[1 - c], ex_rs.at[0, 0])
-    for i in range(NB):
-        gather_start(i, scatter_end(0, i))
+    gather_start(0, scatter_end(0, 0))
+    scatter_mid(0, 1)
+    gather_start(1, scatter_end(0, 1))
     l_wg.wait()
     arrived(wgv.at[1], w_rs.at[1])
     l_wd.wait()
     arrived(wdv.at[1], w_rs.at[2])
-    for i in range(NB):
-        gather_end(i)
-        activate(i)
-        multiply(1, i, hid, wdv, False)
-        scatter_start(1, i)
-    for i in range(NB):
-        finish(i)
+    gather_end(0)
+    activate(0)
+    multiply(1, 0, hid, wdv, False)
+    scatter_start(1, 0)
+    gather_end(1)
+    activate(1)
+    multiply(1, 1, hid, wdv, False)
+    scatter_start(1, 1)
+    finish(0)
+    finish(1)
 
     def rows_of(blocks, k):
         parts = []
@@ -263,7 +299,7 @@
     DMA = pltpu.SemaphoreType.DMA
     att, ffn = pl.pallas_call(
         kernel,
-        out_shape=(jax.ShapeDtypeStruct((8, D), BF), jax.ShapeDtypeStruct((8, D), BF)),
+        out_shape=(V((8, D), BF), V((8, D), BF)),
         in_specs=[anyspec, anyspec, smem, smem] + [anyspec] * 6,
         out_specs=(vmem, vmem),
         scratch_shapes=[
@@ -286,7 +322,7 @@
         out_shape=(jax.ShapeDtypeStruct((8, D), BF), jax.ShapeDtypeStruct((8, D), BF)),
         in_specs=[vmem, vmem],
         out_specs=(vmem, vmem),
-    )(att, ffn)
+    )(pltpu.with_memory_space_constraint(att, pltpu.VMEM), pltpu.with_memory_space_constraint(ffn, pltpu.VMEM))
 
 
 def solution(mesh):

time: 59.9 us -> 57.4 us (0.958)
  Pallas kernels: 59.1 us -> 56.7 us
    pallas_call x1, Pallas kernels: 57.6 us -> 56.1 us  [body(): pl.pallas_call(kernel, out_shape=(V((8, D), BF), V((8, D), BF)), in_specs...]
    pallas_call x1, Pallas kernels: 1.49 us -> 0.65 us  [body(): pl.pallas_call(keep, out_shape=(jax.ShapeDtypeStruct((8, D), BF), jax.Sha...]
where the time goes in v4:
time: 57.4 us
  Pallas kernels  56.7 us (99%)
  between operations  0.64 us (1%)
    pallas_call x1, Pallas kernels, body(): pl.pallas_call(kernel, out_shape=(V((8, D), BF), V((8, D), BF)), in_specs...  56.1 us

profile of v4, /device:TPU:1, one launch (start us, length us, event | category | flops | bytes accessed | tf_op | source)
XLA Modules:
  0.0 57.4 jit_solution(15477763737145152412)
XLA Ops:
  0.6 56.1 %shard_map.113 = (bf16[8,3584]{1,0:T(8,128)(2,1)S(1)}, bf16[8,3584]{1,0:T(8,128)(2,1)S(1)}) custom-call(bf16[8,64,576]{2,1,0:T(8,128)(2,1)} %q_h.1, bf16[16,64,576]{2,1,0:T(8,128)(2,1)} %pool_h.1, s32[2,8]{1,0:T(2,128)} %bitcast.3, s32[8]{0:T(128)} %ln.1, bf16[8,3584]{1,0:T(8,128)(2,1)} %res_h.1, bf16[4,512,128]{2,1,0:T(8,128)(2,1)} %wuv_h.1, ...), custom_call_target="tpu_custom_call" | custom-call | flops 1800000000 | bytes 14400000 | tf_op jit(solution)/shard_map/pallas_call | solution.py:300
  56.7 0.6 %shard_map.114 = (bf16[8,3584]{1,0:T(8,128)(2,1)}, bf16[8,3584]{1,0:T(8,128)(2,1)}) custom-call(bf16[8,3584]{1,0:T(8,128)(2,1)S(1)} %get-tuple-element.4.a, bf16[8,3584]{1,0:T(8,128)(2,1)S(1)} %get-tuple-element.5.b), custom_call_target="tpu_custom_call" | custom-call | tf_op jit(solution)/shard_map/pallas_call | solution.py:320

commit v5 on v4

--- a/solution.py
+++ b/solution.py
@@ -22,9 +22,9 @@
 
 
 def kernel(
-    q_h, pool_h, pt, ln, res_h, wuv_h, wout_h, gain_h, wg_h, wd_h,
+    q_h, pool_h, pt_h, ln_h, res_h, wuv_h, wout_h, gain_h, wg_h, wd_h,
     att_o, ffn_o,
-    qv, poolv, resv, wuvv, woutv, gain1, gain2, gainv, wgv, wdv,
+    pt, ln, qv, poolv, resv, wuvv, woutv, gain1, gain2, gainv, wgv, wdv,
     ctxa, ctxb, rctx, lhs, vals,
     part, rsb, rrb, gown, xin, sq, pre, hid, res_s, res_r, att, fin, outx_r,
     lsem, a2a_s, a2a_r, w_ss, w_rs, v_ss, v_rs, rg_ss, rg_rs, ag_ss, ag_rs, h_ss, h_rs, ex_ss, ex_rs,
@@ -56,6 +56,8 @@
         cp.start()
         return cp
 
+    l_pt = load(pt_h, pt)
+    l_ln = load(ln_h, ln)
     l_q = [load(q_h.at[pl.ds(4 * i, 4)], qv.at[pl.ds(4 * i, 4)]) for i in range(NB)]
     l_pool = load(pool_h, poolv)
     l_res = load(res_h, resv)
@@ -71,6 +73,12 @@
         )
         cp.start()
         sends.append(cp)
+
+    def flush(keep):
+        old = len(sends) - keep
+        for cp in sends[:old]:
+            cp.wait_send()
+        del sends[:old]
 
     def arrived(dst, rs):
         pltpu.make_async_copy(dst, dst, rs).wait()
@@ -214,6 +222,8 @@
     def push(src, dst, n):
         remote(src.at[:, pl.ds(oth_col, HALF)], dst.at[1], w_ss.at[n], w_rs.at[n], other)
 
+    l_pt.wait()
+    l_ln.wait()
     l_pool.wait()
     l_q[0].wait()
     attend(0)
@@ -256,6 +266,7 @@
     arrived(wgv.at[1], w_rs.at[1])
     l_wd.wait()
     arrived(wdv.at[1], w_rs.at[2])
+    flush(16)
     gather_end(0)
     activate(0)
     multiply(1, 0, hid, wdv, False)
@@ -264,6 +275,7 @@
     activate(1)
     multiply(1, 1, hid, wdv, False)
     scatter_start(1, 1)
+    flush(8)
     finish(0)
     finish(1)
 
@@ -282,8 +294,7 @@
             arrived(outx_r.at[t, i], ex_rs.at[t + 1, i])
         for k in (0, 1):
             o[:, pl.ds(pl.multiple_of(oth_col + k * CH, 128), CH)] = rows_of([outx_r[t, i] for i in range(NB)], k)
-    for cp in sends:
-        cp.wait_send()
+    flush(0)
 
 
 def keep(a, b, att_o, ffn_o):
@@ -293,17 +304,16 @@
 
 def body(queries, cache_pool, page_table, lengths, residual, w_uv, w_out, norm_gain, w_gate, w_down):
     anyspec = pl.BlockSpec(memory_space=pl.ANY)
-    smem = pl.BlockSpec(memory_space=pltpu.SMEM)
     vmem = pl.BlockSpec(memory_space=pltpu.VMEM)
     V = pltpu.VMEM
     DMA = pltpu.SemaphoreType.DMA
     att, ffn = pl.pallas_call(
         kernel,
         out_shape=(V((8, D), BF), V((8, D), BF)),
-        in_specs=[anyspec, anyspec, smem, smem] + [anyspec] * 6,
+        in_specs=[anyspec, anyspec, anyspec, anyspec] + [anyspec] * 6,
         out_specs=(vmem, vmem),
         scratch_shapes=[
-            V((8, 64, KW), BF), V((16, 64, KW), BF), V((8, D), BF), V((4, LAT, 128), BF),
+            pltpu.SMEM((2, 8), jnp.int32), pltpu.SMEM((8,), jnp.int32), V((8, 64, KW), BF), V((16, 64, KW), BF), V((8, D), BF), V((4, LAT, 128), BF),
             V((2, 512, HALF), BF), V((D,), F32), V((1, D), F32), V((1, HALF), F32), V((2, FFL, HALF), BF), V((2, FFL, HALF), BF),
             V((NB, 256, LAT), BF), V((NB, 256, LAT), BF), V((NB, Z, 2, 16, LAT), BF), V((NB, 256, LAT), BF), V((NB, 2, 64, 512), BF),
             V((2, NB, 2, 64, CH), F32), V((2, NB, Z, 16, CH), BF), V((2, NB, Z, 16, CH), BF),

time: 57.4 us -> 57.2 us (level)
  no operation moved by 1% of the time
where the time goes in v5:
time: 57.2 us; the launch traced here: 57.1 us
  Pallas kernels  56.5 us (99%)
  between operations  0.64 us (1%)
    pallas_call x1, Pallas kernels, body(): pl.pallas_call(kernel, out_shape=(V((8, D), BF), V((8, D), BF)), in_specs...  55.9 us

profile of v5, /device:TPU:1, one launch (start us, length us, event | category | flops | bytes accessed | tf_op | source)
XLA Modules:
  0.0 57.1 jit_solution(1577128759783312175)
XLA Ops:
  0.6 55.9 %shard_map.113 = (bf16[8,3584]{1,0:T(8,128)(2,1)S(1)}, bf16[8,3584]{1,0:T(8,128)(2,1)S(1)}) custom-call(bf16[8,64,576]{2,1,0:T(8,128)(2,1)} %q_h.1, bf16[16,64,576]{2,1,0:T(8,128)(2,1)} %pool_h.1, s32[2,8]{1,0:T(2,128)} %bitcast.3, s32[8]{0:T(128)} %ln_h.1, bf16[8,3584]{1,0:T(8,128)(2,1)} %res_h.1, bf16[4,512,128]{2,1,0:T(8,128)(2,1)} %wuv_h.1, ...), custom_call_target="tpu_custom_call" | custom-call | flops 1800000000 | bytes 14400000 | tf_op jit(solution)/shard_map/pallas_call | solution.py:310
  56.5 0.6 %shard_map.114 = (bf16[8,3584]{1,0:T(8,128)(2,1)}, bf16[8,3584]{1,0:T(8,128)(2,1)}) custom-call(bf16[8,3584]{1,0:T(8,128)(2,1)S(1)} %get-tuple-element.4.a, bf16[8,3584]{1,0:T(8,128)(2,1)S(1)} %get-tuple-element.5.b), custom_call_target="tpu_custom_call" | custom-call | tf_op jit(solution)/shard_map/pallas_call | solution.py:330

commit v6 on v5

--- a/solution.py
+++ b/solution.py
@@ -236,6 +236,15 @@
     attend(1)
     send_contexts(1)
 
+    l_wuv.wait()
+    l_wout.wait()
+    arrived(woutv.at[1], w_rs.at[0])
+
+    def finish(i):
+        fin[i] = (att[0, i] + scatter_end(1, i)).astype(BF).astype(F32)
+        remote(fin.at[i], outx_r.at[1, i], ex_ss.at[2, i], ex_rs.at[2, i], other)
+
+    project(0)
     l_res.wait()
     res_r[c] = resv[:, pl.ds(own_col, HALF)].astype(F32)
     res_s[...] = resv[:, pl.ds(oth_col, HALF)].astype(F32)
@@ -244,15 +253,6 @@
     gain2[...] = gain1[...].reshape(1, D)
     gainv[...] = gain2[:, pl.ds(own_col, HALF)]
 
-    l_wuv.wait()
-    l_wout.wait()
-    arrived(woutv.at[1], w_rs.at[0])
-
-    def finish(i):
-        fin[i] = (att[0, i] + scatter_end(1, i)).astype(BF).astype(F32)
-        remote(fin.at[i], outx_r.at[1, i], ex_ss.at[2, i], ex_rs.at[2, i], other)
-
-    project(0)
     multiply(0, 0, vals, woutv, True)
     scatter_start(0, 0)
     project(1)

time: 57.2 us -> 56.6 us (0.990)
  Pallas kernels: 56.5 us -> 55.9 us
    pallas_call x1, Pallas kernels: 55.9 us -> 55.3 us  [body(): pl.pallas_call(kernel, out_shape=(V((8, D), BF), V((8, D), BF)), in_specs...]
where the time goes in v6:
time: 56.6 us
  Pallas kernels  55.9 us (99%)
  between operations  0.64 us (1%)
    pallas_call x1, Pallas kernels, body(): pl.pallas_call(kernel, out_shape=(V((8, D), BF), V((8, D), BF)), in_specs...  55.3 us

profile of v6, /device:TPU:1, one launch (start us, length us, event | category | flops | bytes accessed | tf_op | source)
XLA Modules:
  0.0 56.6 jit_solution(9746350668210006689)
XLA Ops:
  0.6 55.3 %shard_map.113 = (bf16[8,3584]{1,0:T(8,128)(2,1)S(1)}, bf16[8,3584]{1,0:T(8,128)(2,1)S(1)}) custom-call(bf16[8,64,576]{2,1,0:T(8,128)(2,1)} %q_h.1, bf16[16,64,576]{2,1,0:T(8,128)(2,1)} %pool_h.1, s32[2,8]{1,0:T(2,128)} %bitcast.3, s32[8]{0:T(128)} %ln_h.1, bf16[8,3584]{1,0:T(8,128)(2,1)} %res_h.1, bf16[4,512,128]{2,1,0:T(8,128)(2,1)} %wuv_h.1, ...), custom_call_target="tpu_custom_call" | custom-call | flops 1800000000 | bytes 14400000 | tf_op jit(solution)/shard_map/pallas_call | solution.py:310
  55.9 0.6 %shard_map.114 = (bf16[8,3584]{1,0:T(8,128)(2,1)}, bf16[8,3584]{1,0:T(8,128)(2,1)}) custom-call(bf16[8,3584]{1,0:T(8,128)(2,1)S(1)} %get-tuple-element.4.a, bf16[8,3584]{1,0:T(8,128)(2,1)S(1)} %get-tuple-element.5.b), custom_call_target="tpu_custom_call" | custom-call | tf_op jit(solution)/shard_map/pallas_call | solution.py:330
